TPU v7x, 512 devices: a whole 4x4x16 slice. The times are simulated.
512 devices in a mesh: gx: 16 (over x, y), gy: 16 (over z_lo, core), var: 2 (over z_hi).
Axes of the slice: x: 4, y: 4, z: 16 (z_hi: 2, z_lo: 8; z = z_hi * 8 + z_lo), core: 2. Of those that a mesh axis runs over, the one named last changes fastest.
Arguments:
- field: bfloat16 [4, 1024, 1024, 128], P('var', 'gx', 'gy'), may hold values from -6 to 6
- probe_first: bfloat16 [1024, 40], P('gx'), may hold values from -0.1875 to 0.1875
- probe_second: bfloat16 [1024, 40], P('gy'), may hold values from -0.1875 to 0.1875
- probe_depth: bfloat16 [128, 40], replicated, may hold values from -0.5 to 0.5
- probe_vars: bfloat16 [4, 40], P('var'), may hold values from -3 to 3
- shrink_first: bfloat16 [48, 1024], P(None, 'gx'), may hold values from -0.25 to 0.25
- shrink_second: bfloat16 [48, 1024], P(None, 'gy'), may hold values from -0.25 to 0.25
- shrink_depth: bfloat16 [48, 128], replicated, may hold values from -0.5 to 0.5
- shrink_vars: bfloat16 [4, 4], P(None, 'var'), may hold values from -4 to 4
Outputs:
- range_first: float32 [1024, 40], P('gx')
- range_second: float32 [1024, 40], P('gy')
- range_depth: float32 [128, 40], replicated
- core_sketch: float32 [4, 48, 48, 48], P('var', 'gx', 'gy')
All inputs are finite; a program needn't handle non-finite values.
Results may differ from a plain program's by a relative error of at most 0.0036.
Values sent between devices are 32-bit elements; how exact they have to be, the bound alone decides.
A program may use at most 64 MiB of HBM per device.

v0:
```python
import jax
import jax.numpy as jnp
from jax import lax
from jax.sharding import PartitionSpec as P

HIGH = lax.Precision.HIGHEST


def on_device(
    field,
    probe_first,
    probe_second,
    probe_depth,
    probe_vars,
    shrink_first,
    shrink_second,
    shrink_depth,
    shrink_vars,
):
    local_vars, rows_first, rows_second, depth = field.shape
    width = probe_depth.shape[1]
    flat = field.reshape(local_vars * rows_first * rows_second, depth)
    joined = jnp.concatenate([probe_depth, shrink_depth.T], axis=1)
    product = jnp.dot(flat, joined, preferred_element_type=jnp.float32)
    probed = product[:, :width].reshape(local_vars, rows_first, rows_second, width)
    compressed = (
        product[:, width:].astype(jnp.bfloat16).reshape(local_vars, rows_first, rows_second, -1)
    )
    first32 = probe_first.astype(jnp.float32)
    second32 = probe_second.astype(jnp.float32)
    var_scale = probe_vars.astype(jnp.float32)
    part_first = jnp.einsum(
        "vijr,vjr->ir", probed, second32[None] * var_scale[:, None, :], precision=HIGH
    )
    part_second = jnp.einsum(
        "vijr,vir->jr", probed, first32[None] * var_scale[:, None, :], precision=HIGH
    )
    tested = (
        first32[None, :, None, :] * second32[None, None, :, :] * var_scale[:, None, None, :]
    ).astype(jnp.bfloat16)
    part_depth = jnp.dot(
        flat.T,
        tested.reshape(local_vars * rows_first * rows_second, width),
        preferred_element_type=jnp.float32,
    )
    range_first = lax.psum(part_first, ("gy", "var"))
    range_second = lax.psum(part_second, ("gx", "var"))
    range_depth = lax.psum(part_depth, ("gx", "gy", "var"))
    mixed = jnp.einsum(
        "ai,vijc->vajc",
        shrink_first.astype(jnp.float32),
        compressed.astype(jnp.float32),
        precision=HIGH,
    )
    core_parts = jnp.einsum(
        "bj,vajc->vabc", shrink_second.astype(jnp.float32), mixed, precision=HIGH
    )
    partial_value = jnp.einsum(
        "wv,vabc->wabc", shrink_vars.astype(jnp.float32), core_parts, precision=HIGH
    )
    reduced = lax.psum_scatter(partial_value, "var", scatter_dimension=0, tiled=True)
    reduced = lax.psum_scatter(reduced, "gx", scatter_dimension=1, tiled=True)
    core_sketch = lax.psum_scatter(reduced, "gy", scatter_dimension=2, tiled=True)
    return (range_first, range_second, range_depth, core_sketch)


def solution(mesh):
    return jax.shard_map(
        on_device,
        mesh=mesh,
        in_specs=(
            P("var", "gx", "gy", None),
            P("gx", None),
            P("gy", None),
            P(),
            P("var", None),
            P(None, "gx"),
            P(None, "gy"),
            P(),
            P(None, "var"),
        ),
        out_specs=(P("gx", None), P("gy", None), P(), P("var", "gx", "gy", None)),
        check_vma=False,
    )
```

profile of v0, /device:TPU:1, one launch (start us, length us, event | category | flops | bytes accessed | tf_op | source)
XLA Modules:
  0.0 1022.5 jit_solution(8216747514507482566)
XLA Ops:
  7.2 1.5 copy-done
  8.8 2.1 convolution_bitcast_fusion
  10.9 1.6 copy-done.1
  12.6 2.6 reshape.32
  15.2 3.2 copy.27
  18.4 3.6 convolution_bitcast_fusion.1
  22.0 4.2 copy.29
  26.2 4.3 fusion.12
  30.5 4.3 copy.31
  34.8 6.5 fusion.2
  41.3 2.5 copy.19
  44.1 215.4 %reduce-scatter.6.cloned.1.call-done = f32[2,48,48,48]{3,2,1,0:T(8,128)} async-done(((f32[4,48,48,48]{3,2,1,0:T(8,128)}), f32[2,48,48,48]{3,2,1,0:T(8,128)}) %reduce-scatter.6.cloned.1.call-update) | async-done | bytes 884752 | tf_op jit(solution)/shard_map/reduce_scatter | solution.py:61
  259.4 3.5 copy.20
  265.0 0.9 copy.22
  266.0 2.5 reshape.31
  268.6 1.3 dynamic-slice.2
  270.5 1.1 broadcast_multiply_fusion
  272.3 122.6 %psum.23 = f32[128,40]{0,1:T(8,128)} all-reduce(f32[128,40]{0,1:T(8,128)S(1)} %fusion.8), channel_id=1, replica_groups=mesh['gx'=16,'gy'=16,'var'=2] {'gx','gy','var'}, use_global_device_ids=true, to_apply=%region_2.0 | all-reduce | flops 5120 | bytes 40960 | tf_op jit(solution)/shard_map/psum | solution.py:48
  394.9 3.9 fusion.17
  398.8 230.4 %psum.21 = f32[64,40]{0,1:T(8,128)} all-reduce(f32[64,40]{0,1:T(8,128)S(1)} %bitcast.68), channel_id=1, replica_groups=mesh['gx'=16,'gy'=16,'var'=2] {'gy','var'}, use_global_device_ids=true, to_apply=%region_0.0 | all-reduce | flops 2560 | bytes 20480 | tf_op jit(solution)/shard_map/psum | solution.py:46
  629.2 4.1 fusion.18
  633.3 269.6 %psum.22 = f32[64,40]{0,1:T(8,128)} all-reduce(f32[64,40]{0,1:T(8,128)S(1)} %bitcast.67), channel_id=1, replica_groups=mesh['gx'=16,'gy'=16,'var'=2] {'gx','var'}, use_global_device_ids=true, to_apply=%region_1.0 | all-reduce | flops 2560 | bytes 20480 | tf_op jit(solution)/shard_map/psum | solution.py:47
  902.9 1.0 copy.21
  903.9 111.2 %all-reduce.1 = f32[2,3,48,48]{3,0,2,1:T(2,128)S(1)} all-reduce(f32[2,3,48,48]{3,0,2,1:T(2,128)S(1)} %copy.21), channel_id=4, replica_groups=mesh['gx'=16,'gy'=16,'var'=2] {'gy'}, use_global_device_ids=true, to_apply=%region_5.0.clone | all-reduce | flops 13824 | bytes 110592
  (30 shorter events, 3.8 us)
Async XLA Ops:
  7.2 1.6 copy-start
  7.2 252.2 %reduce-scatter.6.cloned.1.call-start = ((), (), s32[]{:S(2)}) async-start(), calls=%async_computation.2 | async-start | bytes 7077888 | tf_op jit(solution)/shard_map/reduce_scatter | solution.py:61
  10.9 1.6 copy-start.1
  12.6 5.8 copy-start.3
  22.0 4.2 copy-start.4
  30.5 4.3 copy-start.6
  43.8 859.0 %reduce-scatter.8.cloned.1.call-start = ((), (), s32[]{:S(2)}) async-start(), calls=%async_computation.3 | async-start | bytes 2506752
  262.9 0.7 copy-start.2
  262.9 1.4 copy-start.5
  262.9 1.5 copy-start.7
  262.9 3.1 slice-start
Sparse Core Ops, SparseCore 0:
  44.0 215.4 reduce-scatter.5
  264.2 102.8 reduce-scatter.7
where the time goes:
time: 1030 us; the launch traced here: 1020 us
  blocking collectives  734 us (71%)
  waiting for transfers between devices  215 us (21%)
  local copies, waits for them, and re-layouts  30.7 us (3%)
  matrix products  25.1 us (2%)
  between operations  14.8 us (1%)
    psum x1, blocking collectives, on_device(): range_second = lax.psum(part_second, ('gx', 'var'))  270 us
    psum x1, blocking collectives, on_device(): range_first = lax.psum(part_first, ('gy', 'var'))  230 us
    reduce_scatter x1, waiting for transfers between devices, on_device(): lax.psum_scatter(partial_value, 'var', scatter_dimension=0, tiled=True)  215 us
    psum x1, blocking collectives, on_device(): range_depth = lax.psum(part_depth, ('gx', 'gy', 'var'))  123 us
    unnamed x1, blocking collectives  111 us
  transfers between devices with their start and end apart: 2, of which 1 were waited for; matrix products, arithmetic and copies ran while one was open for 2% of the time, Pallas kernels for 0%

commit v1 on v0

v1 whole, which is shorter than its diff:
```python
import jax
import jax.numpy as jnp
from jax import lax
from jax.experimental import pallas as pl
from jax.experimental.pallas import tpu as pltpu
from jax.sharding import PartitionSpec as P

F32 = jnp.float32
BF16 = jnp.bfloat16
MESH = pl.DeviceIdType.MESH

NX, NY, NZ = 4, 4, 16
GX = NX * NY
HALF = NZ // 2
PLANE = [
    (2, 2), (2, 1), (1, 2), (2, 3), (3, 2), (1, 1), (3, 3), (1, 3), (3, 1),
    (2, 0), (0, 2), (1, 0), (0, 1), (3, 0), (0, 3),
]
LINE = [8, 7, 9, 6, 10, 5, 11, 4, 12, 3, 13, 2, 14, 1, 15]
CHUNKS = 2
ZC = HALF // CHUNKS


def dot(a, b):
    return jnp.dot(a, b, preferred_element_type=F32)


def iota(shape, axis):
    return lax.broadcasted_iota(jnp.int32, shape, axis)


def kernel(
    field,
    probe_first,
    probe_second,
    probe_depth,
    probe_vars,
    shrink_first,
    shrink_second,
    shrink_depth,
    shrink_vars,
    out_first,
    out_second,
    out_depth,
    out_core,
    held,
    pad,
    joined,
    spread,
    mix,
    stage,
    mixed,
    weight_first,
    weight_second,
    tall_first,
    tall_second,
    tall_vars,
    rows_first,
    rows_second,
    core_away,
    core_own,
    core_sib,
    core_sum,
    core_plane,
    core_tiles,
    core_line,
    depth_parts,
    depth_sib,
    depth_sum,
    depth_plane,
    depth_tile,
    depth_line,
    depth_row,
    depth_back,
    first_pack,
    first_sib,
    first_sum,
    first_line,
    first_whole,
    second_pack,
    second_var,
    second_sum,
    second_plane,
    load_sem,
    pair_send,
    pair_recv,
    core_send,
    core_recv,
    plane_send,
    plane_recv,
    line_send,
    line_recv,
    dplane_send,
    dplane_recv,
    dline_send,
    dline_recv,
    drow_send,
    drow_recv,
    fline_send,
    fline_recv,
    splane_send,
    splane_recv,
):
    gx, gy, half = lax.axis_index("gx"), lax.axis_index("gy"), lax.axis_index("var")
    x, y = gx // NY, gx % NY
    z, core = half * HALF + gy // 2, gy % 2

    def in_plane(dx, dy):
        return ((x + dx) % NX) * NY + (y + dy) % NY

    def at_plane(there):
        return (there, gy, half)

    def at_line(there):
        return (gx, (there % HALF) * 2 + core, there // HALF)

    sibling = (gx, gy + 1 - 2 * core, half)
    partner = (gx, gy, 1 - half)

    barrier = pltpu.get_barrier_semaphore()
    for dz in LINE:
        pl.semaphore_signal(barrier, inc=1, device_id=at_line((z + dz) % NZ), device_id_type=MESH)
    for dx, dy in PLANE:
        pl.semaphore_signal(barrier, inc=1, device_id=at_plane(in_plane(dx, dy)), device_id_type=MESH)
    pl.semaphore_signal(barrier, inc=1, device_id=sibling, device_id_type=MESH)

    def load(g):
        rows = pl.ds(g * 8, 8)
        return pltpu.make_async_copy(field.at[:, rows], held.at[:, rows], load_sem.at[g])

    for g in range(8):
        load(g).start()

    def send(src, dst, send_sem, recv_sem, device):
        copy = pltpu.make_async_remote_copy(
            src_ref=src, dst_ref=dst, send_sem=send_sem, recv_sem=recv_sem, device_id=device, device_id_type=MESH
        )
        copy.start()
        return copy

    lane = iota((128, 128), 1)
    row = iota((128, 128), 0)
    zeros = jnp.zeros((128, 128), F32)

    pad[...] = zeros
    pad[0:48, :] = shrink_depth[...].astype(F32)
    pad[48:96, :] = shrink_depth[...].astype(F32)
    turned = pad[...].T
    joined[0:128, 0:128] = jnp.where(lane < 48, turned, 0.0).astype(BF16)
    joined[128:256, 0:128] = jnp.where(lane >= 48, turned, 0.0).astype(BF16)
    pad[...] = zeros
    pad[:, 0:40] = probe_depth[...].astype(F32)
    wide = pad[...]
    joined[0:128, 128:256] = wide.astype(BF16)
    joined[128:256, 128:256] = pltpu.roll(wide, 64, 1).astype(BF16)

    pad[...] = zeros
    pad[0:2, 0:40] = probe_vars[...].astype(F32)
    both = pad[0:8, :]
    vars_row = both[0:1, :] + pltpu.roll(both, 64, 1)[1:2, :]
    tall_vars[0] = jnp.broadcast_to(both[0:1, :], (128, 128)).T[0:40, :]
    tall_vars[1] = jnp.broadcast_to(both[1:2, :], (128, 128)).T[0:40, :]
    pad[...] = zeros
    pad[0:64, 0:40] = probe_first[...].astype(F32)
    wide = pad[0:64, :]
    weight_first[...] = (wide + pltpu.roll(wide, 64, 1)) * vars_row
    tall_first[...] = pad[...].T[0:40, 0:64].astype(BF16)
    pad[...] = zeros
    pad[0:64, 0:40] = probe_second[...].astype(F32)
    pad[64:128, 0:40] = probe_second[...].astype(F32)
    wide = pad[0:64, :]
    weight_second[...] = (wide + pltpu.roll(wide, 64, 1)) * vars_row
    tall_second[...] = pad[...].T[0:40, :]

    for q in range(4):
        pad[...] = zeros
        pad[0:48, 0:64] = shrink_second[...].astype(F32)
        block = pad[0:48, :]
        if q % 2:
            block = pltpu.roll(block, 64, 1)
        spread[q * 48 : q * 48 + 48, (q // 2) * 128 : (q // 2) * 128 + 128] = block.astype(BF16)
        spread[q * 48 : q * 48 + 48, (1 - q // 2) * 128 : (1 - q // 2) * 128 + 128] = jnp.zeros((48, 128), BF16)

    pad[...] = zeros
    pad[0:48, 0:64] = shrink_first[...].astype(F32)
    wide = pad[0:48, :]
    twice = (wide + pltpu.roll(wide, 64, 1)).astype(BF16)
    at = iota((128, 48), 0)
    col = iota((128, 48), 1)
    each = dot(jnp.where(col == 3 * (at // 8) + (at % 8) % 3, 1.0, 0.0).astype(BF16), twice)
    ninth = dot(jnp.where(col == 3 * (at // 8) + 2, 1.0, 0.0).astype(BF16), twice)
    place = row % 8
    left = lane < 64
    third = place // 3
    blocks = [
        jnp.where(third == jnp.where(left, 0, 1), each, 0.0),
        jnp.where(left, jnp.where(third == 2, each, 0.0), jnp.where(place == 0, ninth, 0.0)),
        jnp.where(place == jnp.where(left, 1, 2), ninth, 0.0),
    ]
    for q in range(3):
        mix[:, q * 128 : q * 128 + 128] = blocks[q].astype(BF16)
        mix[:, (q + 3) * 128 : (q + 3) * 128 + 128] = blocks[q].astype(BF16)

    second_pack[32:40, :] = jnp.zeros((8, 128), F32)
    second_pack[32:36, 0:2] = shrink_vars[...].astype(F32)

    def depth_step(g, total):
        load(g).wait()
        lanes = iota((64, 512), 1)
        pick = jnp.where(iota((64, 512), 0) == g * 8 + lanes // 64, 1.0, 0.0).astype(BF16)
        firsts = dot(tall_first[...], pick)
        seconds = tall_second[...]
        product = firsts * jnp.concatenate([seconds] * 4, axis=1)
        for v in range(2):
            scale = jnp.concatenate([tall_vars[v]] * 4, axis=1)
            tested = (product * scale).astype(BF16)
            total = total + dot(tested, held[v, pl.ds(g * 8, 8)].reshape(512, 128))
        return total

    depth_total = lax.fori_loop(0, 8, depth_step, jnp.zeros((40, 128), F32))
    depth_parts[...] = jnp.zeros((8, 8, 128), F32)
    for g in range(8):
        depth_parts[g, 0:5, :] = depth_total[5 * g : 5 * g + 5, :]

    def field_step(g, total):
        rows = pl.ds(g * 8, 8)
        flat = jnp.concatenate([held[0, rows].reshape(512, 128), held[1, rows].reshape(512, 128)], axis=1)
        product = dot(flat, joined[...])
        compressed = product[:, 0:128].astype(BF16)
        probed = product[:, 128:256].reshape(8, 64, 128)
        for q in range(2):
            stage[pl.ds(pl.multiple_of(g * 384 + q * 192, 64), 192), :] = dot(
                spread[...], compressed[q * 256 : q * 256 + 256, :]
            )
        firsts = weight_first[rows, :]
        seconds = weight_second[...]
        sums = []
        for i in range(8):
            total = total + probed[i] * firsts[i : i + 1, :]
            sums.append(jnp.sum(probed[i] * seconds, axis=0, keepdims=True))
        rows_first[rows, :] = jnp.concatenate(sums, axis=0)
        return total

    rows_second[...] = lax.fori_loop(0, 8, field_step, jnp.zeros((64, 128), F32))

    def pack(rows):
        rows = rows + pltpu.roll(rows, 64, 1)
        return jnp.where(iota((32, 128), 1) < 64, rows[0:32], rows[32:64])

    first_pack[...] = pack(rows_first[...]).reshape(2, 16, 128)
    second_pack[0:32, :] = pack(rows_second[...])

    def core_step(side, target):
        def body(s, _):
            for t in range(2):
                for b in range(3):
                    part = stage[pl.ds((s * 2 + t) * 6 + 3 * side + b, 64, stride=48), :]
                    parts = [(b, part)]
                    if b == 2:
                        for u in range(3):
                            moved = pltpu.roll(part, 96 - 32 * u, 1)
                            parts.append((3 + u, jnp.where(iota((64, 128), 1) >= 96, moved, 0.0)))
                    for at, value in parts:
                        high = value.astype(BF16)
                        low = (value - high.astype(F32)).astype(BF16)
                        mixed[at * 64 : at * 64 + 64, t * 128 : t * 128 + 128] = high
                        mixed[384 + at * 64 : 384 + at * 64 + 64, t * 128 : t * 128 + 128] = low
            result = dot(mix[...], mixed[...])
            for t in range(2):
                to = s * 2 + t
                target[to // ZC, :, to % ZC] = result[:, t * 128 : t * 128 + 128].reshape(GX, 8, 128)
            return 0

        lax.fori_loop(0, 4, body, 0)

    core_step(1 - core, core_away)

    pl.semaphore_wait(barrier, len(LINE) + len(PLANE) + 1)

    waits = []
    there = 1 - core
    pair_depth = send(
        depth_parts.at[pl.ds(there * 4, 4)], depth_sib, pair_send.at[0], pair_recv.at[0], sibling
    )
    pair_first = send(first_pack.at[there], first_sib, pair_send.at[1], pair_recv.at[1], sibling)
    pair_core = [
        send(core_away.at[q], core_sib.at[q], core_send.at[q], core_recv.at[q], sibling) for q in range(CHUNKS)
    ]
    pair_var = send(second_pack, second_var, pair_send.at[2], pair_recv.at[2], partner)
    core_step(core, core_own)

    pair_depth.wait_recv()
    depth_sum[...] = depth_parts[pl.ds(core * 4, 4)] + depth_sib[...]
    for i, (dx, dy) in enumerate(PLANE):
        to = in_plane(dx, dy)
        waits.append(
            send(depth_sum.at[to // NY], depth_plane.at[gx], dplane_send.at[i], dplane_recv.at[gx], at_plane(to))
        )
    depth_plane[gx] = depth_sum[x]

    pair_first.wait_recv()
    first_sum[...] = first_pack[core] + first_sib[...]
    for i, dz in enumerate(LINE):
        waits.append(
            send(first_sum, first_line.at[z], fline_send.at[i], fline_recv.at[z], at_line((z + dz) % NZ))
        )
    first_line[z] = first_sum[...]

    for q in range(CHUNKS):
        pair_core[q].wait_recv()
        core_sum[q] = core_own[q] + core_sib[q]
        for i, (dx, dy) in enumerate(PLANE):
            to = in_plane(dx, dy)
            waits.append(
                send(
                    core_sum.at[q, to],
                    core_plane.at[q, gx],
                    plane_send.at[q, i],
                    plane_recv.at[q, gx],
                    at_plane(to),
                )
            )
        core_plane[q, gx] = core_sum[q, gx]

    def received(dst, sem):
        pltpu.make_async_remote_copy(
            src_ref=dst, dst_ref=dst, send_sem=sem, recv_sem=sem, device_id=sibling, device_id_type=MESH
        ).wait_recv()

    for dx, dy in PLANE:
        of = in_plane(dx, dy)
        received(depth_plane.at[of], dplane_recv.at[of])
    depth_tile[...] = jnp.sum(depth_plane[...], axis=0)
    for i, dz in enumerate(LINE):
        waits.append(
            send(depth_tile, depth_line.at[z], dline_send.at[i], dline_recv.at[z], at_line((z + dz) % NZ))
        )
    depth_line[z] = depth_tile[...]

    pair_var.wait_recv()
    second_sum[...] = second_pack[0:32, :] + second_var[0:32, :]
    for i, (dx, dy) in enumerate(PLANE):
        waits.append(
            send(second_sum, second_plane.at[gx], splane_send.at[i], splane_recv.at[gx], at_plane(in_plane(dx, dy)))
        )
    second_plane[gx] = second_sum[...]

    for q in range(CHUNKS):
        for dx, dy in PLANE:
            of = in_plane(dx, dy)
            received(core_plane.at[q, of], plane_recv.at[q, of])
        core_tiles[q * ZC : q * ZC + ZC] = jnp.sum(core_plane[q], axis=0)
    for i, dz in enumerate(LINE):
        to = (z + dz) % NZ
        waits.append(send(core_tiles.at[to % HALF], core_line.at[z], line_send.at[i], line_recv.at[z], at_line(to)))
    core_line[z] = core_tiles[z % HALF]

    for dz in LINE:
        of = (z + dz) % NZ
        received(depth_line.at[of], dline_recv.at[of])
    depth_row[x] = jnp.sum(depth_line[...], axis=0)
    for i, dx in enumerate((2, 1, 3)):
        waits.append(
            send(
                depth_row.at[x], depth_row.at[x], drow_send.at[i], drow_recv.at[x], at_plane(in_plane(dx, 0))
            )
        )

    for dz in LINE:
        of = (z + dz) % NZ
        received(first_line.at[of], fline_recv.at[of])
    first_whole[core] = jnp.sum(first_line[...], axis=0)
    back_first = send(
        first_whole.at[core], first_whole.at[core], pair_send.at[3], pair_recv.at[3], sibling
    )

    for dx in (2, 1, 3):
        of = (x + dx) % NX
        received(depth_row.at[of], drow_recv.at[of])
    back_depth = send(depth_row, depth_back, pair_send.at[4], pair_recv.at[4], sibling)

    def unpack(packed):
        return packed[:, 0:40], pltpu.roll(packed, 64, 1)[:, 0:40]

    for dx, dy in PLANE:
        of = in_plane(dx, dy)
        received(second_plane.at[of], splane_recv.at[of])
    low, high = unpack(jnp.sum(second_plane[...], axis=0))
    out_second[0:32, :] = low
    out_second[32:64, :] = high

    for dz in LINE:
        of = (z + dz) % NZ
        received(core_line.at[of], line_recv.at[of])
    own, other = second_pack[32:40, 0:2], second_var[32:40, 0:2]
    own, other = jnp.where(half == 0, own[0:2], own[2:4]), jnp.where(half == 0, other[0:2], other[2:4])
    scales = (jnp.where(half == 0, own, other), jnp.where(half == 0, other, own))
    result = [jnp.zeros((8, 48), F32), jnp.zeros((8, 48), F32)]
    last = [jnp.zeros((1, 48), F32), jnp.zeros((1, 48), F32)]
    for h in range(2):
        tile = jnp.sum(core_line[h * HALF : h * HALF + HALF], axis=0)
        lanes = iota((1, 128), 1)
        ninth = jnp.where(
            lanes < 32,
            pltpu.roll(tile, 32, 1)[0:1],
            jnp.where(lanes < 64, pltpu.roll(tile, 64, 1)[1:2], pltpu.roll(tile, 96, 1)[2:3]),
        )
        ninth = jnp.broadcast_to(ninth, (8, 128))
        for v in range(2):
            tile_v = (pltpu.roll(tile, 80, 1) if v else tile)[:, 0:48]
            ninth_v = (pltpu.roll(ninth, 80, 1) if v else ninth)[0:1, 0:48]
            for w in range(2):
                scale = scales[h][w : w + 1, v : v + 1]
                result[w] = result[w] + scale * tile_v
                last[w] = last[w] + scale * ninth_v
    for w in range(2):
        for at in range(9):
            out_core[w, at % 3, at // 3 : at // 3 + 1, :] = result[w][at : at + 1, :] if at < 8 else last[w]

    back_first.wait_recv()
    low, high = unpack(first_whole[...].reshape(32, 128))
    out_first[0:32, :] = low
    out_first[32:64, :] = high

    back_depth.wait_recv()
    mine, theirs = depth_row[...], depth_back[...]
    firsts = jnp.where(core == 0, mine, theirs)
    seconds = jnp.where(core == 0, theirs, mine)
    pad[...] = zeros
    for g in range(4):
        pad[5 * g : 5 * g + 5, :] = firsts[g, 0:5, :]
        pad[20 + 5 * g : 25 + 5 * g, :] = seconds[g, 0:5, :]
    out_depth[...] = pad[...].T[:, 0:40]

    for copy in waits + pair_core + [pair_depth, pair_first, pair_var, back_first, back_depth]:
        copy.wait_send()


def on_device(*args):
    vmem = pl.BlockSpec(memory_space=pltpu.VMEM)
    dma = pltpu.SemaphoreType.DMA
    return pl.pallas_call(
        kernel,
        name="tucker",
        out_shape=(
            jax.ShapeDtypeStruct((64, 40), F32),
            jax.ShapeDtypeStruct((64, 40), F32),
            jax.ShapeDtypeStruct((128, 40), F32),
            jax.ShapeDtypeStruct((2, 3, 3, 48), F32),
        ),
        in_specs=[pl.BlockSpec(memory_space=pl.ANY)] + [vmem] * 8,
        out_specs=(vmem,) * 4,
        scratch_shapes=[
            pltpu.VMEM((2, 64, 64, 128), BF16),
            pltpu.VMEM((128, 128), F32),
            pltpu.VMEM((256, 256), BF16),
            pltpu.VMEM((192, 256), BF16),
            pltpu.VMEM((128, 768), BF16),
            pltpu.VMEM((64 * 48, 128), F32),
            pltpu.VMEM((768, 256), BF16),
            pltpu.VMEM((64, 128), F32),
            pltpu.VMEM((64, 128), F32),
            pltpu.VMEM((40, 64), BF16),
            pltpu.VMEM((40, 128), F32),
            pltpu.VMEM((2, 40, 128), F32),
            pltpu.VMEM((64, 128), F32),
            pltpu.VMEM((64, 128), F32),
            pltpu.VMEM((CHUNKS, GX, ZC, 8, 128), F32),
            pltpu.VMEM((CHUNKS, GX, ZC, 8, 128), F32),
            pltpu.VMEM((CHUNKS, GX, ZC, 8, 128), F32),
            pltpu.VMEM((CHUNKS, GX, ZC, 8, 128), F32),
            pltpu.VMEM((CHUNKS, GX, ZC, 8, 128), F32),
            pltpu.VMEM((HALF, 8, 128), F32),
            pltpu.VMEM((NZ, 8, 128), F32),
            pltpu.VMEM((8, 8, 128), F32),
            pltpu.VMEM((4, 8, 128), F32),
            pltpu.VMEM((4, 8, 128), F32),
            pltpu.VMEM((GX, 8, 128), F32),
            pltpu.VMEM((8, 128), F32),
            pltpu.VMEM((NZ, 8, 128), F32),
            pltpu.VMEM((NX, 8, 128), F32),
            pltpu.VMEM((NX, 8, 128), F32),
            pltpu.VMEM((2, 16, 128), F32),
            pltpu.VMEM((16, 128), F32),
            pltpu.VMEM((16, 128), F32),
            pltpu.VMEM((NZ, 16, 128), F32),
            pltpu.VMEM((2, 16, 128), F32),
            pltpu.VMEM((40, 128), F32),
            pltpu.VMEM((40, 128), F32),
            pltpu.VMEM((32, 128), F32),
            pltpu.VMEM((GX, 32, 128), F32),
            dma((8,)),
            dma((5,)),
            dma((5,)),
            dma((CHUNKS,)),
            dma((CHUNKS,)),
            dma((CHUNKS, 15)),
            dma((CHUNKS, GX)),
            dma((15,)),
            dma((NZ,)),
            dma((15,)),
            dma((GX,)),
            dma((15,)),
            dma((NZ,)),
            dma((3,)),
            dma((NX,)),
            dma((15,)),
            dma((NZ,)),
            dma((15,)),
            dma((GX,)),
        ],
        compiler_params=pltpu.CompilerParams(
            collective_id=0, has_side_effects=True, vmem_limit_bytes=32 << 20
        ),
        cost_estimate=pl.CostEstimate(flops=2_000_000_000, bytes_accessed=3_000_000, transcendentals=0),
    )(*args)


def solution(mesh):
    return jax.shard_map(
        on_device,
        mesh=mesh,
        in_specs=(
            P("var", "gx", "gy", None),
            P("gx", None),
            P("gy", None),
            P(),
            P("var", None),
            P(None, "gx"),
            P(None, "gy"),
            P(),
            P(None, "var"),
        ),
        out_specs=(P("gx", None), P("gy", None), P(), P("var", "gx", "gy", None)),
        check_vma=False,
    )
```

time: 1030 us -> 53.4 us (0.05)
  blocking collectives: 734 us -> 0 us
  waiting for transfers between devices: 215 us -> 0 us
  Pallas kernels: 0 us -> 42 us
  matrix products: 25.1 us -> 0 us
  local copies, waits for them, and re-layouts: 30.7 us -> 10.2 us
  between operations: 14.8 us -> 0.65 us
    psum x3 -> x0, blocking collectives: 623 us -> none  [the longest x1 270 us: on_device(): range_second = lax.psum(part_second, ('gx', 'var'))]
    reduce_scatter x1 -> x0, waiting for transfers between devices: 215 us -> none  [on_device(): lax.psum_scatter(partial_value, 'var', scatter_dimension=0, tiled=True)]
    unnamed x1 -> x0, blocking collectives: 111 us -> none
    pallas_call x0 -> x1, Pallas kernels: none -> 42 us  [on_device(): pl.pallas_call(kernel, name='tucker', out_shape=(jax.ShapeDtypeStruct((64...]
    dot_general x7 -> x0, matrix products: 25.1 us -> none  [the longest x1 6.51 us: on_device(): jnp.einsum('wv,vabc->wabc', shrink_vars.astype(jnp.float32), core_parts,...]
  transfers between devices with their start and end apart: 2 -> 0, of which waited for: 1 -> 0; matrix products, arithmetic and copies ran while one was open for 2% -> 0% of each run, Pallas kernels for 0% -> 0%
where the time goes in v1:
time: 53.4 us; the launch traced here: 52.8 us
  Pallas kernels  42 us (79%)
  local copies, waits for them, and re-layouts  10.2 us (19%)
  between operations  0.65 us (1%)
    pallas_call x1, Pallas kernels, on_device(): pl.pallas_call(kernel, name='tucker', out_shape=(jax.ShapeDtypeStruct((64...  42 us
    unnamed x14, local copies, waits for them, and re-layouts  7.53 us
    pallas_call x4, local copies, waits for them, and re-layouts, on_device(): pl.pallas_call(kernel, name='tucker', out_shape=(jax.ShapeDtypeStruct((64...  2.65 us

profile of v1, /device:TPU:1, one launch (start us, length us, event | category | flops | bytes accessed | tf_op | source)
XLA Modules:
  0.0 52.8 jit_solution(17483159908782635312)
XLA Ops:
  0.6 0.8 %copy.16.shrink_vars = bf16[4,2]{1,0:T(4,128)(2,1)S(1)} copy(bf16[4,2]{0,1:T(2,128)(2,1)} %param.17) | data formatting | bytes 32 | tf_op args[8]
  1.4 0.8 %copy.13.probe_first = bf16[64,40]{1,0:T(8,128)(2,1)S(1)} copy(bf16[64,40]{0,1:T(8,128)(2,1)} %param.10) | data formatting | bytes 10240 | tf_op args[1]
  2.2 0.8 %copy.14.probe_second = bf16[64,40]{1,0:T(8,128)(2,1)S(1)} copy(bf16[64,40]{0,1:T(8,128)(2,1)} %param.11) | data formatting | bytes 10240 | tf_op args[2]
  3.0 0.8 %copy.15.probe_depth = bf16[128,40]{1,0:T(8,128)(2,1)S(1)} copy(bf16[128,40]{0,1:T(8,128)(2,1)} %param.12) | data formatting | bytes 20480 | tf_op args[3]
  3.8 0.0 copy-start
  3.8 1.6 %copy-done = bf16[2,64,64,128]{3,2,1,0:T(8,128)(2,1)S(1)} copy-done((bf16[2,64,64,128]{3,2,1,0:T(8,128)(2,1)S(1)}, bf16[2,64,64,128]{3,2,1,0:T(8,128)(2,1)}, u32[]{:S(2)}) %copy-start) | copy-done | bytes 2097176
  5.4 0.0 copy-start.1
  5.4 0.7 %copy-done.1 = bf16[48,64]{1,0:T(8,128)(2,1)S(1)} copy-done((bf16[48,64]{1,0:T(8,128)(2,1)S(1)}, bf16[48,64]{1,0:T(8,128)(2,1)}, u32[]{:S(2)}) %copy-start.1) | copy-done | bytes 6168
  6.1 0.0 copy-start.2
  6.1 0.7 %copy-done.2 = bf16[48,64]{1,0:T(8,128)(2,1)S(1)} copy-done((bf16[48,64]{1,0:T(8,128)(2,1)S(1)}, bf16[48,64]{1,0:T(8,128)(2,1)}, u32[]{:S(2)}) %copy-start.2) | copy-done | bytes 6168
  6.8 0.0 copy-start.3
  6.8 0.7 %copy-done.3 = bf16[48,128]{1,0:T(8,128)(2,1)S(1)} copy-done((bf16[48,128]{1,0:T(8,128)(2,1)S(1)}, bf16[48,128]{1,0:T(8,128)(2,1)}, u32[]{:S(2)}) %copy-start.3) | copy-done | bytes 12312
  7.5 0.0 copy-start.4
  7.5 0.7 %copy-done.4 = bf16[2,40]{1,0:T(2,128)(2,1)S(1)} copy-done((bf16[2,40]{1,0:T(2,128)(2,1)S(1)}, bf16[2,40]{1,0:T(2,128)(2,1)}, u32[]{:S(2)}) %copy-start.4) | copy-done | bytes 184
  8.2 42.0 %tucker.1 = (f32[64,40]{1,0:T(8,128)S(1)}, f32[64,40]{1,0:T(8,128)S(1)}, f32[128,40]{1,0:T(8,128)S(1)}, f32[2,3,3,48]{3,2,1,0:T(4,128)S(1)}) custom-call(bf16[2,64,64,128]{3,2,1,0:T(8,128)(2,1)S(1)} %copy-done, bf16[64,40]{1,0:T(8,128)(2,1)S(1)} %copy.13.probe_first, bf16[64,40]{1,0:T(8,128)(2,1)S(1)} %copy.14.probe_second, ...), custom_call_target="tpu_custom_call" | custom-call | flops 2000000000 | bytes 3000000 | tf_op jit(solution)/shard_map/tucker/pallas_call | solution.py:442
  50.1 0.7 %copy.17 = f32[64,40]{0,1:T(8,128)} copy(f32[64,40]{1,0:T(8,128)S(1)} %get-tuple-element.4) | data formatting | bytes 20480 | tf_op jit(solution)/shard_map/tucker/pallas_call | solution.py:442
  50.8 0.6 %copy.20 = f32[2,3,3,48]{3,0,2,1:T(2,128)} copy(f32[2,3,3,48]{3,2,1,0:T(4,128)S(1)} %get-tuple-element.7) | data formatting | bytes 6912 | tf_op jit(solution)/shard_map/tucker/pallas_call | solution.py:442
  51.4 0.7 %copy.18 = f32[64,40]{0,1:T(8,128)} copy(f32[64,40]{1,0:T(8,128)S(1)} %get-tuple-element.5) | data formatting | bytes 20480 | tf_op jit(solution)/shard_map/tucker/pallas_call | solution.py:442
  52.1 0.7 %copy.19 = f32[128,40]{0,1:T(8,128)} copy(f32[128,40]{1,0:T(8,128)S(1)} %get-tuple-element.6) | data formatting | bytes 40960 | tf_op jit(solution)/shard_map/tucker/pallas_call | solution.py:442
Async XLA Ops:
  3.8 1.6 %copy-start = (bf16[2,64,64,128]{3,2,1,0:T(8,128)(2,1)S(1)}, bf16[2,64,64,128]{3,2,1,0:T(8,128)(2,1)}, u32[]{:S(2)}) copy-start(bf16[2,64,64,128]{3,2,1,0:T(8,128)(2,1)} %field.1) | copy-start | bytes 6291460
  5.4 0.7 %copy-start.1 = (bf16[48,64]{1,0:T(8,128)(2,1)S(1)}, bf16[48,64]{1,0:T(8,128)(2,1)}, u32[]{:S(2)}) copy-start(bf16[48,64]{1,0:T(8,128)(2,1)} %shrink_first.1) | copy-start | bytes 18436
  6.1 0.7 %copy-start.2 = (bf16[48,64]{1,0:T(8,128)(2,1)S(1)}, bf16[48,64]{1,0:T(8,128)(2,1)}, u32[]{:S(2)}) copy-start(bf16[48,64]{1,0:T(8,128)(2,1)} %shrink_second.1) | copy-start | bytes 18436
  6.8 0.7 %copy-start.3 = (bf16[48,128]{1,0:T(8,128)(2,1)S(1)}, bf16[48,128]{1,0:T(8,128)(2,1)}, u32[]{:S(2)}) copy-start(bf16[48,128]{1,0:T(8,128)(2,1)} %shrink_depth.1) | copy-start | bytes 36868
  7.5 0.7 %copy-start.4 = (bf16[2,40]{1,0:T(2,128)(2,1)S(1)}, bf16[2,40]{1,0:T(2,128)(2,1)}, u32[]{:S(2)}) copy-start(bf16[2,40]{1,0:T(2,128)(2,1)} %probe_vars.1) | copy-start | bytes 484

commit v2 on v1

v2 whole, which is shorter than its diff:
```python
import jax
import jax.numpy as jnp
from jax import lax
from jax.experimental import pallas as pl
from jax.experimental.pallas import tpu as pltpu
from jax.sharding import PartitionSpec as P

F32 = jnp.float32
BF16 = jnp.bfloat16
MESH = pl.DeviceIdType.MESH

NX, NY, NZ = 4, 4, 16
GX = NX * NY
HALF = NZ // 2
PLANE = [
    (2, 2), (2, 1), (1, 2), (2, 3), (3, 2), (1, 1), (3, 3), (1, 3), (3, 1),
    (2, 0), (0, 2), (1, 0), (0, 1), (3, 0), (0, 3),
]
ROW = [(2, 0), (2, 1), (1, 0), (3, 0), (1, 1), (3, 1), (0, 1)]
LINE = [8, 7, 9, 6, 10, 5, 11, 4, 12, 3, 13, 2, 14, 1, 15]
CHUNKS = 2
ZC = HALF // CHUNKS
OFFSET = 2
LOADS = 4


def dot(a, b):
    return jnp.dot(a, b, preferred_element_type=F32)


def iota(shape, axis):
    return lax.broadcasted_iota(jnp.int32, shape, axis)


def kernel(
    field,
    probe_first_hbm,
    probe_second_hbm,
    probe_depth_hbm,
    probe_vars_hbm,
    shrink_first_hbm,
    shrink_second_hbm,
    shrink_depth_hbm,
    shrink_vars_hbm,
    out_first,
    out_second,
    out_depth,
    out_core,
    probe_first,
    probe_second,
    probe_depth,
    probe_vars,
    shrink_first,
    shrink_second,
    shrink_depth,
    shrink_vars,
    held,
    pad,
    joined,
    spread,
    mix,
    stage,
    mixed,
    tested,
    weight_first,
    weight_second,
    rows_first,
    rows_second,
    core_away,
    core_own,
    core_sib,
    core_sum,
    core_plane,
    core_tiles,
    core_line,
    depth_parts,
    depth_sib,
    depth_sum,
    depth_plane,
    depth_tile,
    depth_line,
    depth_all,
    first_pack,
    first_sib,
    first_sum,
    first_line,
    first_whole,
    second_pack,
    second_var,
    second_sum,
    second_plane,
    small_sem,
    load_sem,
    pair_send,
    pair_recv,
    core_send,
    core_recv,
    plane_send,
    plane_recv,
    many_send,
    many_recv,
):
    gx, gy, half = lax.axis_index("gx"), lax.axis_index("gy"), lax.axis_index("var")
    x, y = gx // NY, gx % NY
    z_low, core = gy // 2, gy % 2
    z = half * HALF + z_low

    def in_plane(dx, dy):
        return ((x + dx) % NX) * NY + (y + dy) % NY

    def at_plane(there):
        return (there, gy, half)

    def at_line(there):
        return (gx, (there % HALF) * 2 + core, there // HALF)

    sibling = (gx, gy + 1 - 2 * core, half)
    partner = (gx, gy, 1 - half)
    row_peers = [(in_plane(dx, 0), gy + turn * (1 - 2 * core), half) for dx, turn in ROW]

    small = [
        pltpu.make_async_copy(src, dst, small_sem.at[i])
        for i, (src, dst) in enumerate(
            (
                (probe_first_hbm, probe_first),
                (probe_second_hbm, probe_second),
                (probe_vars_hbm, probe_vars),
                (probe_depth_hbm, probe_depth),
                (shrink_depth_hbm, shrink_depth),
                (shrink_second_hbm, shrink_second),
                (shrink_first_hbm, shrink_first),
                (shrink_vars_hbm, shrink_vars),
            )
        )
    ]
    for copy in small:
        copy.start()

    def load(part):
        rows = pl.ds(part * (64 // LOADS), 64 // LOADS)
        return pltpu.make_async_copy(field.at[:, rows], held.at[:, rows], load_sem.at[part])

    for part in range(LOADS):
        load(part).start()

    barrier = pltpu.get_barrier_semaphore()
    for dz in LINE:
        pl.semaphore_signal(barrier, inc=1, device_id=at_line((z + dz) % NZ), device_id_type=MESH)
    for dx, dy in PLANE:
        pl.semaphore_signal(barrier, inc=1, device_id=at_plane(in_plane(dx, dy)), device_id_type=MESH)
    for device, (dx, turn) in zip(row_peers, ROW):
        if turn:
            pl.semaphore_signal(barrier, inc=1, device_id=device, device_id_type=MESH)

    def send(src, dst, send_sem, recv_sem, device):
        copy = pltpu.make_async_remote_copy(
            src_ref=src, dst_ref=dst, send_sem=send_sem, recv_sem=recv_sem, device_id=device, device_id_type=MESH
        )
        copy.start()
        return copy

    def all_of(ref, sem):
        return pltpu.make_async_remote_copy(
            src_ref=ref, dst_ref=ref, send_sem=sem, recv_sem=sem, device_id=sibling, device_id_type=MESH
        )

    lane = iota((128, 128), 1)
    row = iota((128, 128), 0)
    zeros = jnp.zeros((128, 128), F32)

    for copy in small:
        copy.wait()

    def twice_turned(rows, offset):
        count, length = rows.shape
        pad[...] = zeros
        pad[0:count, 0:length] = rows
        pad[offset : offset + count, 0:length] = rows
        return pad[...].T

    pad[...] = zeros
    pad[0:2, 0:40] = probe_vars[...].astype(F32)
    both = pad[0:8, :]
    vars_row = both[0:1, :] + pltpu.roll(both, 64, 1)[1:2, :]
    tall = jnp.where(row < 64, both[0:1, :], both[1:2, :]).T[0:40, :]
    turned = pltpu.roll(tall, 64, 1)
    tall_vars = (
        jnp.where(iota((40, 128), 1) < 64, tall, turned),
        jnp.where(iota((40, 128), 1) < 64, turned, tall),
    )
    pad[...] = zeros
    pad[0:40, 0:64] = probe_second[...].astype(F32)
    wide = pad[0:40, :]
    tall_second = wide + pltpu.roll(wide, 64, 1)
    for g in range(8):
        lanes = iota((64, 512), 1)
        pick = jnp.where(iota((64, 512), 0) == g * 8 + lanes // 64, 1.0, 0.0).astype(BF16)
        firsts = dot(probe_first[...], pick)
        for q in range(4):
            product = firsts[:, q * 128 : q * 128 + 128] * tall_second
            for v in range(2):
                tested[v, :, g * 512 + q * 128 : g * 512 + q * 128 + 128] = (product * tall_vars[v]).astype(BF16)

    weight_first[...] = twice_turned(probe_first[...].astype(F32), 64)[0:64, :] * vars_row
    weight_second[...] = twice_turned(probe_second[...].astype(F32), 64)[0:64, :] * vars_row
    wide = twice_turned(probe_depth[...].astype(F32), 64)
    joined[0:128, 128:256] = jnp.where(lane < 64, wide, 0.0).astype(BF16)
    joined[128:256, 128:256] = jnp.where(lane >= 64, wide, 0.0).astype(BF16)
    wide = twice_turned(shrink_depth[...].astype(F32), 48)
    joined[0:128, 0:128] = jnp.where(lane < 48, wide, 0.0).astype(BF16)
    joined[128:256, 0:128] = jnp.where(lane >= 48, wide, 0.0).astype(BF16)

    pad[...] = zeros
    pad[0:48, 0:64] = shrink_second[...].astype(F32)
    block = pad[0:48, :]
    turned = pltpu.roll(block, 64, 1).astype(BF16)
    block = block.astype(BF16)
    for q in range(4):
        here, there = (q // 2) * 128, (1 - q // 2) * 128
        spread[q * 48 : q * 48 + 48, here : here + 128] = turned if q % 2 else block
        spread[q * 48 : q * 48 + 48, there : there + 128] = jnp.zeros((48, 128), BF16)

    pad[...] = zeros
    pad[0:48, 0:64] = shrink_first[...].astype(F32)
    wide = pad[0:48, :]
    twice = (wide + pltpu.roll(wide, 64, 1)).astype(BF16)
    at = iota((128, 48), 0)
    col = iota((128, 48), 1)
    each = dot(jnp.where(col == 3 * (at // 8) + (at % 8) % 3, 1.0, 0.0).astype(BF16), twice)
    ninth = dot(jnp.where(col == 3 * (at // 8) + 2, 1.0, 0.0).astype(BF16), twice)
    place = row % 8
    left = lane < 64
    third = place // 3
    blocks = [
        jnp.where(third == jnp.where(left, 0, 1), each, 0.0),
        jnp.where(left, jnp.where(third == 2, each, 0.0), jnp.where(place == 0, ninth, 0.0)),
        jnp.where(place == jnp.where(left, 1, 2), ninth, 0.0),
    ]
    for q in range(3):
        mix[:, q * 128 : q * 128 + 128] = blocks[q].astype(BF16)
        mix[:, (q + 3) * 128 : (q + 3) * 128 + 128] = blocks[q].astype(BF16)

    second_pack[...] = jnp.zeros((32, 128), F32)
    first_pack[...] = jnp.zeros((2, 16, 128), F32)
    second_pack[24:26, 0:4] = shrink_vars[...].astype(F32)
    depth_parts[...] = jnp.zeros((8, 8, 128), F32)

    depth_total = jnp.zeros((40, 128), F32)
    step = 64 // LOADS
    for part in range(LOADS):
        load(part).wait()
        for v in range(2):
            depth_total = depth_total + dot(
                tested[v, :, part * step * 64 : (part + 1) * step * 64],
                held[v, part * step : (part + 1) * step].reshape(step * 64, 128),
            )
    for g in range(8):
        depth_parts[g, 0:5, :] = depth_total[5 * g : 5 * g + 5, :]

    pl.semaphore_wait(barrier, len(LINE) + len(PLANE) + 4)

    pair_depth = send(
        depth_parts.at[pl.ds((1 - core) * 4, 4)], depth_sib, pair_send.at[0], pair_recv.at[0], sibling
    )

    def field_step(g, total):
        flat = jnp.concatenate(
            [held[v, g * 8 : g * 8 + 8].reshape(512, 128) for v in range(2)], axis=1
        )
        product = dot(flat, joined[...])
        compressed = product[:, 0:128].astype(BF16)
        probed = product[:, 128:256].reshape(8, 64, 128)
        for q in range(2):
            stage[g * 384 + q * 192 : g * 384 + q * 192 + 192, :] = dot(
                spread[...], compressed[q * 256 : q * 256 + 256, :]
            )
        firsts = weight_first[g * 8 : g * 8 + 8, :]
        seconds = weight_second[...]
        sums = []
        for i in range(8):
            total = total + probed[i] * firsts[i : i + 1, :]
            sums.append(jnp.sum(probed[i] * seconds, axis=0, keepdims=True))
        rows_first[g * 8 : g * 8 + 8, :] = jnp.concatenate(sums, axis=0)
        return total

    second_total = jnp.zeros((64, 128), F32)
    for g in range(4):
        second_total = field_step(g, second_total)

    pair_depth.wait_recv()
    depth_sum[...] = depth_parts[pl.ds(core * 4, 4)] + depth_sib[...]
    for dx, dy in PLANE:
        to = in_plane(dx, dy)
        send(depth_sum.at[to // NY], depth_plane.at[gx], many_send.at[0], many_recv.at[0], at_plane(to))
    depth_plane[gx] = depth_sum[x]

    for g in range(4, 8):
        second_total = field_step(g, second_total)
    rows_second[...] = second_total

    def pack(rows):
        rows = rows + pltpu.roll(rows, 64, 1)
        pad[0:64, :] = rows
        pad[64:128, :] = pltpu.roll(rows, 108, 1)
        return pad[...].T[0:20, :]

    packed = pack(rows_first[...])
    first_pack[0, 0:10, :] = packed[0:10, :]
    first_pack[1, 0:10, :] = packed[10:20, :]
    second_pack[0:20, :] = pack(rows_second[...])

    pair_first = send(first_pack.at[1 - core], first_sib, pair_send.at[1], pair_recv.at[1], sibling)
    pair_var = send(second_pack, second_var, pair_send.at[2], pair_recv.at[2], partner)

    def core_step(side, target, q):
        for s in range(ZC // 2):
            for t in range(2):
                place = (z_low + HALF - OFFSET + q * ZC + s * 2 + t) % HALF
                for b in range(3):
                    part = stage[pl.ds(place * 6 + 3 * side + b, 64, stride=48), :]
                    parts = [(b, part)]
                    if b == 2:
                        for u in range(3):
                            moved = pltpu.roll(part, 96 - 32 * u, 1)
                            parts.append((3 + u, jnp.where(iota((64, 128), 1) >= 96, moved, 0.0)))
                    for at, value in parts:
                        high = value.astype(BF16)
                        low = (value - high.astype(F32)).astype(BF16)
                        mixed[s, at * 64 : at * 64 + 64, t * 128 : t * 128 + 128] = high
                        mixed[s, 384 + at * 64 : 384 + at * 64 + 64, t * 128 : t * 128 + 128] = low
            result = dot(mix[...], mixed[s])
            for t in range(2):
                target[q, :, s * 2 + t] = result[:, t * 128 : t * 128 + 128].reshape(GX, 8, 128)

    pair_core = []
    for q in range(CHUNKS):
        core_step(1 - core, core_away, q)
        pair_core.append(send(core_away.at[q], core_sib.at[q], core_send.at[q], core_recv.at[q], sibling))
    for q in range(CHUNKS):
        core_step(core, core_own, q)

    for q in range(CHUNKS):
        pair_core[q].wait_recv()
        core_sum[q] = core_own[q] + core_sib[q]
        for dx, dy in PLANE:
            to = in_plane(dx, dy)
            send(core_sum.at[q, to], core_plane.at[q, gx], plane_send.at[q], plane_recv.at[q], at_plane(to))
        core_plane[q, gx] = core_sum[q, gx]

    pair_first.wait_recv()
    first_sum[...] = first_pack[core] + first_sib[...]
    for dz in LINE:
        send(
            first_sum.at[pl.ds(0, 8)],
            first_line.at[z],
            many_send.at[1],
            many_recv.at[1],
            at_line((z + dz) % NZ),
        )
    first_line[z] = first_sum[0:8, :]

    all_of(depth_plane.at[pl.ds(0, 15)], many_recv.at[0]).wait_recv()
    depth_tile[0:5, :] = jnp.sum(depth_plane[...], axis=0)[0:5, :]
    depth_tile[5:8, :] = first_sum[8:11, :]
    for dz in LINE:
        send(depth_tile, depth_line.at[z], many_send.at[2], many_recv.at[2], at_line((z + dz) % NZ))
    depth_line[z] = depth_tile[...]

    for q in range(CHUNKS):
        all_of(core_plane.at[q, pl.ds(0, 15)], plane_recv.at[q]).wait_recv()
        core_tiles[q] = jnp.sum(core_plane[q], axis=0)
        for far in (0, 1):
            for s in range(ZC):
                ahead = q * ZC + s - OFFSET
                if ahead == 0 and far:
                    continue
                to = (z + ahead + HALF * (1 - far) + NZ) % NZ
                send(core_tiles.at[q, s], core_line.at[z], many_send.at[3], many_recv.at[3], at_line(to))
        if q == 0:
            core_line[z] = core_tiles[0, OFFSET]
            pair_var.wait_recv()
            second_sum[...] = second_pack[0:24, :] + second_var[0:24, :]
            for dx, dy in PLANE:
                send(
                    second_sum,
                    second_plane.at[gx],
                    many_send.at[4],
                    many_recv.at[4],
                    at_plane(in_plane(dx, dy)),
                )
            second_plane[gx] = second_sum[...]

    mine = core * NX + x
    all_of(depth_line.at[pl.ds(0, 15)], many_recv.at[2]).wait_recv()
    depth_line_sum = jnp.sum(depth_line[...], axis=0)
    depth_all[mine] = depth_line_sum
    for device in row_peers:
        send(depth_all.at[mine], depth_all.at[mine], many_send.at[5], many_recv.at[5], device)

    all_of(first_line.at[pl.ds(0, 15)], many_recv.at[1]).wait_recv()
    first_whole[core, 0:8, :] = jnp.sum(first_line[...], axis=0)
    first_whole[core, 8:16, :] = pltpu.roll(depth_line_sum, 3, 0)
    back_first = send(
        first_whole.at[core], first_whole.at[core], pair_send.at[3], pair_recv.at[3], sibling
    )

    all_of(second_plane.at[pl.ds(0, 15)], many_recv.at[4]).wait_recv()
    packed = jnp.sum(second_plane[...], axis=0)
    out_second[0:20, :] = packed[0:20, 0:64]
    out_second[20:40, :] = pltpu.roll(packed, 64, 1)[0:20, 0:64]

    all_of(core_line.at[pl.ds(0, 15)], many_recv.at[3]).wait_recv()
    own, other = second_pack[24:32, 0:4], second_var[24:32, 0:4]
    own = jnp.where(half == 0, own[0:2, 0:2], own[0:2, 2:4])
    other = jnp.where(half == 0, other[0:2, 0:2], other[0:2, 2:4])
    scales = (jnp.where(half == 0, own, other), jnp.where(half == 0, other, own))
    result = [jnp.zeros((8, 48), F32), jnp.zeros((8, 48), F32)]
    last = [jnp.zeros((1, 48), F32), jnp.zeros((1, 48), F32)]
    for h in range(2):
        tile = jnp.sum(core_line[h * HALF : h * HALF + HALF], axis=0)
        lanes = iota((1, 128), 1)
        ninth = jnp.where(
            lanes < 32,
            pltpu.roll(tile, 32, 1)[0:1],
            jnp.where(lanes < 64, pltpu.roll(tile, 64, 1)[1:2], pltpu.roll(tile, 96, 1)[2:3]),
        )
        ninth = jnp.broadcast_to(ninth, (8, 128))
        for v in range(2):
            tile_v = (pltpu.roll(tile, 80, 1) if v else tile)[:, 0:48]
            ninth_v = (pltpu.roll(ninth, 80, 1) if v else ninth)[0:1, 0:48]
            for w in range(2):
                scale = scales[h][v : v + 1, w : w + 1]
                result[w] = result[w] + scale * tile_v
                last[w] = last[w] + scale * ninth_v
    for w in range(2):
        for at in range(9):
            out_core[at % 3, at // 3, w : w + 1, :] = result[w][at : at + 1, :] if at < 8 else last[w]

    back_first.wait_recv()
    for c in range(2):
        half_rows = first_whole[c]
        out_first[c * 10 : c * 10 + 10, :] = half_rows[0:10, 0:64]
        out_first[20 + c * 10 : 30 + c * 10, :] = pltpu.roll(half_rows, 64, 1)[0:10, 0:64]

    all_of(depth_all.at[pl.ds(0, 7)], many_recv.at[5]).wait_recv()
    for g in range(8):
        out_depth[5 * g : 5 * g + 5, :] = depth_all[g, 0:5, :]

    for copy in pair_core + [pair_depth, pair_first, pair_var, back_first]:
        copy.wait_send()
    for q in range(CHUNKS):
        all_of(core_sum.at[q, pl.ds(0, 15)], plane_send.at[q]).wait_send()
    for i, ref in enumerate((depth_plane, first_line, depth_line, core_line, second_plane)):
        all_of(ref.at[pl.ds(0, 15)], many_send.at[i]).wait_send()
    all_of(depth_all.at[pl.ds(0, 7)], many_send.at[5]).wait_send()


def finish(*refs):
    for i in range(4):
        refs[4 + i][...] = refs[i][...]


def on_device(
    field,
    probe_first,
    probe_second,
    probe_depth,
    probe_vars,
    shrink_first,
    shrink_second,
    shrink_depth,
    shrink_vars,
):
    vmem = pl.BlockSpec(memory_space=pltpu.VMEM)
    dma = pltpu.SemaphoreType.DMA
    shapes = (
        jax.ShapeDtypeStruct((40, 64), F32),
        jax.ShapeDtypeStruct((40, 64), F32),
        jax.ShapeDtypeStruct((40, 128), F32),
        jax.ShapeDtypeStruct((3, 3, 2, 48), F32),
    )
    results = pl.pallas_call(
        kernel,
        name="tucker",
        out_shape=shapes,
        in_specs=[pl.BlockSpec(memory_space=pltpu.HBM)] * 9,
        out_specs=(vmem,) * 4,
        scratch_shapes=[
            pltpu.VMEM((40, 64), BF16),
            pltpu.VMEM((40, 64), BF16),
            pltpu.VMEM((40, 128), BF16),
            pltpu.VMEM((2, 40), BF16),
            pltpu.VMEM((48, 64), BF16),
            pltpu.VMEM((48, 64), BF16),
            pltpu.VMEM((48, 128), BF16),
            pltpu.VMEM((2, 4), BF16),
            pltpu.VMEM((2, 64, 64, 128), BF16),
            pltpu.VMEM((128, 128), F32),
            pltpu.VMEM((256, 256), BF16),
            pltpu.VMEM((192, 256), BF16),
            pltpu.VMEM((128, 768), BF16),
            pltpu.VMEM((64 * 48, 128), F32),
            pltpu.VMEM((ZC // 2, 768, 256), BF16),
            pltpu.VMEM((2, 40, 4096), BF16),
            pltpu.VMEM((64, 128), F32),
            pltpu.VMEM((64, 128), F32),
            pltpu.VMEM((64, 128), F32),
            pltpu.VMEM((64, 128), F32),
            pltpu.VMEM((CHUNKS, GX, ZC, 8, 128), F32),
            pltpu.VMEM((CHUNKS, GX, ZC, 8, 128), F32),
            pltpu.VMEM((CHUNKS, GX, ZC, 8, 128), F32),
            pltpu.VMEM((CHUNKS, GX, ZC, 8, 128), F32),
            pltpu.VMEM((CHUNKS, GX, ZC, 8, 128), F32),
            pltpu.VMEM((CHUNKS, ZC, 8, 128), F32),
            pltpu.VMEM((NZ, 8, 128), F32),
            pltpu.VMEM((8, 8, 128), F32),
            pltpu.VMEM((4, 8, 128), F32),
            pltpu.VMEM((4, 8, 128), F32),
            pltpu.VMEM((GX, 8, 128), F32),
            pltpu.VMEM((8, 128), F32),
            pltpu.VMEM((NZ, 8, 128), F32),
            pltpu.VMEM((8, 8, 128), F32),
            pltpu.VMEM((2, 16, 128), F32),
            pltpu.VMEM((16, 128), F32),
            pltpu.VMEM((16, 128), F32),
            pltpu.VMEM((NZ, 8, 128), F32),
            pltpu.VMEM((2, 16, 128), F32),
            pltpu.VMEM((32, 128), F32),
            pltpu.VMEM((32, 128), F32),
            pltpu.VMEM((24, 128), F32),
            pltpu.VMEM((GX, 24, 128), F32),
            dma((8,)),
            dma((LOADS,)),
            dma((4,)),
            dma((4,)),
            dma((CHUNKS,)),
            dma((CHUNKS,)),
            dma((CHUNKS,)),
            dma((CHUNKS,)),
            dma((6,)),
            dma((6,)),
        ],
        compiler_params=pltpu.CompilerParams(
            collective_id=0, has_side_effects=True, vmem_limit_bytes=60 << 20
        ),
        cost_estimate=pl.CostEstimate(flops=2_000_000_000, bytes_accessed=3_000_000, transcendentals=0),
    )(
        field,
        probe_first.T,
        probe_second.T,
        probe_depth.T,
        probe_vars,
        shrink_first,
        shrink_second,
        shrink_depth,
        shrink_vars.T,
    )
    first, second, depth, core = pl.pallas_call(
        finish,
        name="finish",
        out_shape=shapes,
        in_specs=[vmem] * 4,
        out_specs=(vmem,) * 4,
        compiler_params=pltpu.CompilerParams(vmem_limit_bytes=60 << 20),
    )(*results)
    return first.T, second.T, depth.T, core.transpose(2, 0, 1, 3)


def solution(mesh):
    return jax.shard_map(
        on_device,
        mesh=mesh,
        in_specs=(
            P("var", "gx", "gy", None),
            P("gx", None),
            P("gy", None),
            P(),
            P("var", None),
            P(None, "gx"),
            P(None, "gy"),
            P(),
            P(None, "var"),
        ),
        out_specs=(P("gx", None), P("gy", None), P(), P("var", "gx", "gy", None)),
        check_vma=False,
    )
```

time: 53.4 us -> 38.6 us (0.72)
  local copies, waits for them, and re-layouts: 10.2 us -> 0 us
  Pallas kernels: 42 us -> 37.8 us
    unnamed x14 -> x0, local copies, waits for them, and re-layouts: 7.53 us -> none
    pallas_call x1 -> x2, Pallas kernels: 42 us -> 37.8 us  [the longest x1 36.4 us: on_device(): pl.pallas_call(kernel, name='tucker', out_shape=shapes, in_specs=[pl.Bloc...]
    pallas_call x4 -> x0, local copies, waits for them, and re-layouts: 2.65 us -> none  [on_device(): pl.pallas_call(kernel, name='tucker', out_shape=(jax.ShapeDtypeStruct((64...]
where the time goes in v2:
time: 38.6 us; the launch traced here: 38.4 us
  Pallas kernels  37.8 us (98%)
  between operations  0.64 us (2%)
    pallas_call x1, Pallas kernels, on_device(): pl.pallas_call(kernel, name='tucker', out_shape=shapes, in_specs=[pl.Bloc...  36.4 us
    pallas_call x1, Pallas kernels, on_device(): pl.pallas_call(finish, name='finish', out_shape=shapes, in_specs=[vmem] *...  1.39 us

profile of v2, /device:TPU:1, one launch (start us, length us, event | category | flops | bytes accessed | tf_op | source)
XLA Modules:
  0.0 38.4 jit_solution(11200402749173295254)
XLA Ops:
  0.6 36.4 %tucker.1 = (f32[40,64]{1,0:T(8,128)}, f32[40,64]{1,0:T(8,128)}, f32[40,128]{1,0:T(8,128)}, f32[3,3,2,48]{3,2,1,0:T(2,128)}) custom-call(bf16[2,64,64,128]{3,2,1,0:T(8,128)(2,1)} %field.1, bf16[40,64]{1,0:T(8,128)(2,1)} %bitcast.11, bf16[40,64]{1,0:T(8,128)(2,1)} %bitcast.12, bf16[40,128]{1,0:T(8,128)(2,1)} %bitcast.13, bf16[2,40]{1,0:T(2,128)(2,1)} %probe_vars_hbm.1, ...), custom_call_target="tpu_custom_call" | custom-call | flops 2000000000 | bytes 3000000 | tf_op jit(solution)/shard_map/tucker/pallas_call | solution.py:482
  37.0 1.4 %finish.1 = (f32[40,64]{1,0:T(8,128)}, f32[40,64]{1,0:T(8,128)}, f32[40,128]{1,0:T(8,128)}, f32[3,3,2,48]{3,2,1,0:T(2,128)}) custom-call(f32[40,64]{1,0:T(8,128)} %get-tuple-element.12.refs_0_, f32[40,64]{1,0:T(8,128)} %get-tuple-element.13.refs_1_, f32[40,128]{1,0:T(8,128)} %get-tuple-element.14.refs_2_, f32[3,3,2,48]{3,2,1,0:T(2,128)} %get-tuple-element.15.refs_3_), custom_call_target="tpu_custom_call" | custom-call | tf_op jit(solution)/shard_map/finish/pallas_call | solution.py:558

commit v3 on v2

--- a/solution.py
+++ b/solution.py
@@ -22,6 +22,7 @@
 ZC = HALF // CHUNKS
 OFFSET = 2
 LOADS = 4
+BEFORE = 7
 
 
 def dot(a, b):
@@ -227,22 +228,25 @@
     at = iota((128, 48), 0)
     col = iota((128, 48), 1)
     each = dot(jnp.where(col == 3 * (at // 8) + (at % 8) % 3, 1.0, 0.0).astype(BF16), twice)
-    ninth = dot(jnp.where(col == 3 * (at // 8) + 2, 1.0, 0.0).astype(BF16), twice)
+    folded = dot(jnp.where(col == 3 * (at // 8) + 1 + (at % 8) // 3, 1.0, 0.0).astype(BF16), twice)
     place = row % 8
     left = lane < 64
     third = place // 3
+    whole = place < 7
+    short = place < 6
+    turn = place % 3
     blocks = [
-        jnp.where(third == jnp.where(left, 0, 1), each, 0.0),
-        jnp.where(left, jnp.where(third == 2, each, 0.0), jnp.where(place == 0, ninth, 0.0)),
-        jnp.where(place == jnp.where(left, 1, 2), ninth, 0.0),
+        jnp.where(whole & (third == jnp.where(left, 0, 1)), each, 0.0),
+        jnp.where(left, jnp.where(place == 6, each, 0.0), jnp.where(short & (turn == 0), folded, 0.0)),
+        jnp.where(short & (turn == jnp.where(left, 1, 2)), folded, 0.0),
     ]
     for q in range(3):
         mix[:, q * 128 : q * 128 + 128] = blocks[q].astype(BF16)
         mix[:, (q + 3) * 128 : (q + 3) * 128 + 128] = blocks[q].astype(BF16)
 
-    second_pack[...] = jnp.zeros((32, 128), F32)
+    second_pack[...] = jnp.zeros((24, 128), F32)
     first_pack[...] = jnp.zeros((2, 16, 128), F32)
-    second_pack[24:26, 0:4] = shrink_vars[...].astype(F32)
+    second_pack[20:22, 0:4] = shrink_vars[...].astype(F32)
     depth_parts[...] = jnp.zeros((8, 8, 128), F32)
 
     depth_total = jnp.zeros((40, 128), F32)
@@ -256,12 +260,6 @@
             )
     for g in range(8):
         depth_parts[g, 0:5, :] = depth_total[5 * g : 5 * g + 5, :]
-
-    pl.semaphore_wait(barrier, len(LINE) + len(PLANE) + 4)
-
-    pair_depth = send(
-        depth_parts.at[pl.ds((1 - core) * 4, 4)], depth_sib, pair_send.at[0], pair_recv.at[0], sibling
-    )
 
     def field_step(g, total):
         flat = jnp.concatenate(
@@ -284,7 +282,16 @@
         return total
 
     second_total = jnp.zeros((64, 128), F32)
-    for g in range(4):
+    for g in range(BEFORE):
+        second_total = field_step(g, second_total)
+
+    pl.semaphore_wait(barrier, len(LINE) + len(PLANE) + 4)
+
+    pair_depth = send(
+        depth_parts.at[pl.ds((1 - core) * 4, 4)], depth_sib, pair_send.at[0], pair_recv.at[0], sibling
+    )
+
+    for g in range(BEFORE, BEFORE + 1):
         second_total = field_step(g, second_total)
 
     pair_depth.wait_recv()
@@ -294,7 +301,7 @@
         send(depth_sum.at[to // NY], depth_plane.at[gx], many_send.at[0], many_recv.at[0], at_plane(to))
     depth_plane[gx] = depth_sum[x]
 
-    for g in range(4, 8):
+    for g in range(BEFORE + 1, 8):
         second_total = field_step(g, second_total)
     rows_second[...] = second_total
 
@@ -309,8 +316,8 @@
     first_pack[1, 0:10, :] = packed[10:20, :]
     second_pack[0:20, :] = pack(rows_second[...])
 
+    pair_var = send(second_pack, second_var, pair_send.at[2], pair_recv.at[2], partner)
     pair_first = send(first_pack.at[1 - core], first_sib, pair_send.at[1], pair_recv.at[1], sibling)
-    pair_var = send(second_pack, second_var, pair_send.at[2], pair_recv.at[2], partner)
 
     def core_step(side, target, q):
         for s in range(ZC // 2):
@@ -335,7 +342,13 @@
     pair_core = []
     for q in range(CHUNKS):
         core_step(1 - core, core_away, q)
-        pair_core.append(send(core_away.at[q], core_sib.at[q], core_send.at[q], core_recv.at[q], sibling))
+        pair_core.append(send(
+                core_away.at[q, :, :, pl.ds(0, 7)],
+                core_sib.at[q, :, :, pl.ds(0, 7)],
+                core_send.at[q],
+                core_recv.at[q],
+                sibling,
+            ))
     for q in range(CHUNKS):
         core_step(core, core_own, q)
 
@@ -344,7 +357,13 @@
         core_sum[q] = core_own[q] + core_sib[q]
         for dx, dy in PLANE:
             to = in_plane(dx, dy)
-            send(core_sum.at[q, to], core_plane.at[q, gx], plane_send.at[q], plane_recv.at[q], at_plane(to))
+            send(
+                core_sum.at[q, to, :, pl.ds(0, 7)],
+                core_plane.at[q, gx, :, pl.ds(0, 7)],
+                plane_send.at[q],
+                plane_recv.at[q],
+                at_plane(to),
+            )
         core_plane[q, gx] = core_sum[q, gx]
 
     pair_first.wait_recv()
@@ -367,7 +386,7 @@
     depth_line[z] = depth_tile[...]
 
     for q in range(CHUNKS):
-        all_of(core_plane.at[q, pl.ds(0, 15)], plane_recv.at[q]).wait_recv()
+        all_of(core_plane.at[q, pl.ds(0, 15), :, pl.ds(0, 7)], plane_recv.at[q]).wait_recv()
         core_tiles[q] = jnp.sum(core_plane[q], axis=0)
         for far in (0, 1):
             for s in range(ZC):
@@ -379,7 +398,7 @@
         if q == 0:
             core_line[z] = core_tiles[0, OFFSET]
             pair_var.wait_recv()
-            second_sum[...] = second_pack[0:24, :] + second_var[0:24, :]
+            second_sum[...] = second_pack[...] + second_var[...]
             for dx, dy in PLANE:
                 send(
                     second_sum,
@@ -410,31 +429,35 @@
     out_second[20:40, :] = pltpu.roll(packed, 64, 1)[0:20, 0:64]
 
     all_of(core_line.at[pl.ds(0, 15)], many_recv.at[3]).wait_recv()
-    own, other = second_pack[24:32, 0:4], second_var[24:32, 0:4]
+    own, other = second_pack[16:24, 0:4][4:6], second_var[16:24, 0:4][4:6]
     own = jnp.where(half == 0, own[0:2, 0:2], own[0:2, 2:4])
     other = jnp.where(half == 0, other[0:2, 0:2], other[0:2, 2:4])
     scales = (jnp.where(half == 0, own, other), jnp.where(half == 0, other, own))
     result = [jnp.zeros((8, 48), F32), jnp.zeros((8, 48), F32)]
-    last = [jnp.zeros((1, 48), F32), jnp.zeros((1, 48), F32)]
+    last = [jnp.zeros((8, 48), F32), jnp.zeros((8, 48), F32)]
+    lanes = iota((8, 128), 1)
     for h in range(2):
         tile = jnp.sum(core_line[h * HALF : h * HALF + HALF], axis=0)
-        lanes = iota((1, 128), 1)
-        ninth = jnp.where(
+        folded = jnp.where(
             lanes < 32,
-            pltpu.roll(tile, 32, 1)[0:1],
-            jnp.where(lanes < 64, pltpu.roll(tile, 64, 1)[1:2], pltpu.roll(tile, 96, 1)[2:3]),
+            pltpu.roll(tile, 32, 1),
+            jnp.where(
+                lanes < 64,
+                pltpu.roll(pltpu.roll(tile, 64, 1), 7, 0),
+                pltpu.roll(pltpu.roll(tile, 96, 1), 6, 0),
+            ),
         )
-        ninth = jnp.broadcast_to(ninth, (8, 128))
         for v in range(2):
             tile_v = (pltpu.roll(tile, 80, 1) if v else tile)[:, 0:48]
-            ninth_v = (pltpu.roll(ninth, 80, 1) if v else ninth)[0:1, 0:48]
+            folded_v = (pltpu.roll(folded, 80, 1) if v else folded)[:, 0:48]
             for w in range(2):
                 scale = scales[h][v : v + 1, w : w + 1]
                 result[w] = result[w] + scale * tile_v
-                last[w] = last[w] + scale * ninth_v
+                last[w] = last[w] + scale * folded_v
     for w in range(2):
         for at in range(9):
-            out_core[at % 3, at // 3, w : w + 1, :] = result[w][at : at + 1, :] if at < 8 else last[w]
+            source, of = (result[w], at) if at < 7 else (last[w], 3 * (at - 7))
+            out_core[at % 3, at // 3, w : w + 1, :] = source[of : of + 1, :]
 
     back_first.wait_recv()
     for c in range(2):
@@ -449,7 +472,7 @@
     for copy in pair_core + [pair_depth, pair_first, pair_var, back_first]:
         copy.wait_send()
     for q in range(CHUNKS):
-        all_of(core_sum.at[q, pl.ds(0, 15)], plane_send.at[q]).wait_send()
+        all_of(core_sum.at[q, pl.ds(0, 15), :, pl.ds(0, 7)], plane_send.at[q]).wait_send()
     for i, ref in enumerate((depth_plane, first_line, depth_line, core_line, second_plane)):
         all_of(ref.at[pl.ds(0, 15)], many_send.at[i]).wait_send()
     all_of(depth_all.at[pl.ds(0, 7)], many_send.at[5]).wait_send()
@@ -525,8 +548,8 @@
             pltpu.VMEM((16, 128), F32),
             pltpu.VMEM((NZ, 8, 128), F32),
             pltpu.VMEM((2, 16, 128), F32),
-            pltpu.VMEM((32, 128), F32),
-            pltpu.VMEM((32, 128), F32),
+            pltpu.VMEM((24, 128), F32),
+            pltpu.VMEM((24, 128), F32),
             pltpu.VMEM((24, 128), F32),
             pltpu.VMEM((GX, 24, 128), F32),
             dma((8,)),

time: 38.6 us -> 36.7 us (0.951)
  Pallas kernels: 37.8 us -> 35.8 us
    pallas_call x1, Pallas kernels: 36.4 us -> 34.4 us  [on_device(): pl.pallas_call(kernel, name='tucker', out_shape=shapes, in_specs=[pl.Bloc...]
where the time goes in v3:
time: 36.7 us; the launch traced here: 36.5 us
  Pallas kernels  35.8 us (98%)
  between operations  0.64 us (2%)
    pallas_call x1, Pallas kernels, on_device(): pl.pallas_call(kernel, name='tucker', out_shape=shapes, in_specs=[pl.Bloc...  34.4 us
    pallas_call x1, Pallas kernels, on_device(): pl.pallas_call(finish, name='finish', out_shape=shapes, in_specs=[vmem] *...  1.39 us

profile of v3, /device:TPU:1, one launch (start us, length us, event | category | flops | bytes accessed | tf_op | source)
XLA Modules:
  0.0 36.5 jit_solution(6773417722537111311)
XLA Ops:
  0.6 34.4 %tucker.1 = (f32[40,64]{1,0:T(8,128)}, f32[40,64]{1,0:T(8,128)}, f32[40,128]{1,0:T(8,128)}, f32[3,3,2,48]{3,2,1,0:T(2,128)}) custom-call(bf16[2,64,64,128]{3,2,1,0:T(8,128)(2,1)} %field.1, bf16[40,64]{1,0:T(8,128)(2,1)} %bitcast.11, bf16[40,64]{1,0:T(8,128)(2,1)} %bitcast.12, bf16[40,128]{1,0:T(8,128)(2,1)} %bitcast.13, bf16[2,40]{1,0:T(2,128)(2,1)} %probe_vars_hbm.1, ...), custom_call_target="tpu_custom_call" | custom-call | flops 2000000000 | bytes 3000000 | tf_op jit(solution)/shard_map/tucker/pallas_call | solution.py:505
  35.1 1.4 %finish.1 = (f32[40,64]{1,0:T(8,128)}, f32[40,64]{1,0:T(8,128)}, f32[40,128]{1,0:T(8,128)}, f32[3,3,2,48]{3,2,1,0:T(2,128)}) custom-call(f32[40,64]{1,0:T(8,128)} %get-tuple-element.12.refs_0_, f32[40,64]{1,0:T(8,128)} %get-tuple-element.13.refs_1_, f32[40,128]{1,0:T(8,128)} %get-tuple-element.14.refs_2_, f32[3,3,2,48]{3,2,1,0:T(2,128)} %get-tuple-element.15.refs_3_), custom_call_target="tpu_custom_call" | custom-call | tf_op jit(solution)/shard_map/finish/pallas_call | solution.py:581

commit v4 on v3

--- a/solution.py
+++ b/solution.py
@@ -20,9 +20,8 @@
 LINE = [8, 7, 9, 6, 10, 5, 11, 4, 12, 3, 13, 2, 14, 1, 15]
 CHUNKS = 2
 ZC = HALF // CHUNKS
-OFFSET = 2
 LOADS = 4
-BEFORE = 7
+BEFORE = 3
 
 
 def dot(a, b):
@@ -75,8 +74,6 @@
     core_tiles,
     core_line,
     depth_parts,
-    depth_sib,
-    depth_sum,
     depth_plane,
     depth_tile,
     depth_line,
@@ -115,6 +112,7 @@
     def at_line(there):
         return (gx, (there % HALF) * 2 + core, there // HALF)
 
+    mine = core * NX + x
     sibling = (gx, gy + 1 - 2 * core, half)
     partner = (gx, gy, 1 - half)
     row_peers = [(in_plane(dx, 0), gy + turn * (1 - 2 * core), half) for dx, turn in ROW]
@@ -149,9 +147,9 @@
         pl.semaphore_signal(barrier, inc=1, device_id=at_line((z + dz) % NZ), device_id_type=MESH)
     for dx, dy in PLANE:
         pl.semaphore_signal(barrier, inc=1, device_id=at_plane(in_plane(dx, dy)), device_id_type=MESH)
-    for device, (dx, turn) in zip(row_peers, ROW):
-        if turn:
-            pl.semaphore_signal(barrier, inc=1, device_id=device, device_id_type=MESH)
+        other = (in_plane(dx, dy), gy + 1 - 2 * core, half)
+        pl.semaphore_signal(barrier, inc=1, device_id=other, device_id_type=MESH)
+    pl.semaphore_signal(barrier, inc=1, device_id=sibling, device_id_type=MESH)
 
     def send(src, dst, send_sem, recv_sem, device):
         copy = pltpu.make_async_remote_copy(
@@ -261,47 +259,69 @@
     for g in range(8):
         depth_parts[g, 0:5, :] = depth_total[5 * g : 5 * g + 5, :]
 
+    early = half == 0
+
+    def meet():
+        pl.semaphore_wait(barrier, len(LINE) + 2 * len(PLANE) + 1)
+
+        for dx, dy in PLANE:
+            to = in_plane(dx, dy)
+            for turn in (0, 1):
+                there = core + turn * (1 - 2 * core)
+                send(
+                    depth_parts.at[there * NX + to // NY],
+                    depth_plane.at[core * GX + gx],
+                    many_send.at[0],
+                    many_recv.at[0],
+                    (to, gy + turn * (1 - 2 * core), half),
+                )
+        send(
+            depth_parts.at[(1 - core) * NX + x],
+            depth_plane.at[core * GX + gx],
+            many_send.at[0],
+            many_recv.at[0],
+            sibling,
+        )
+        depth_plane[core * GX + gx] = depth_parts[mine]
+
+    def share():
+        send(second_pack, second_var, pair_send.at[1], pair_recv.at[1], partner)
+        send(first_pack.at[1 - core], first_sib, pair_send.at[0], pair_recv.at[0], sibling)
+
+    def away(q):
+        send(
+            core_away.at[q, :, :, pl.ds(0, 7)],
+            core_sib.at[q, :, :, pl.ds(0, 7)],
+            core_send.at[q],
+            core_recv.at[q],
+            sibling,
+        )
+
+    def rows_of(g):
+        return jnp.concatenate([held[v, g * 16 : g * 16 + 16].reshape(1024, 128) for v in range(2)], axis=1)
+
     def field_step(g, total):
-        flat = jnp.concatenate(
-            [held[v, g * 8 : g * 8 + 8].reshape(512, 128) for v in range(2)], axis=1
-        )
-        product = dot(flat, joined[...])
+        product = dot(rows_of(g), joined[...])
         compressed = product[:, 0:128].astype(BF16)
-        probed = product[:, 128:256].reshape(8, 64, 128)
-        for q in range(2):
-            stage[g * 384 + q * 192 : g * 384 + q * 192 + 192, :] = dot(
+        probed = product[:, 128:256].reshape(16, 64, 128)
+        for q in range(4):
+            stage[g * 768 + q * 192 : g * 768 + q * 192 + 192, :] = dot(
                 spread[...], compressed[q * 256 : q * 256 + 256, :]
             )
-        firsts = weight_first[g * 8 : g * 8 + 8, :]
+        firsts = weight_first[g * 16 : g * 16 + 16, :]
         seconds = weight_second[...]
         sums = []
-        for i in range(8):
+        for i in range(16):
             total = total + probed[i] * firsts[i : i + 1, :]
             sums.append(jnp.sum(probed[i] * seconds, axis=0, keepdims=True))
-        rows_first[g * 8 : g * 8 + 8, :] = jnp.concatenate(sums, axis=0)
+        rows_first[g * 16 : g * 16 + 16, :] = jnp.concatenate(sums, axis=0)
         return total
 
     second_total = jnp.zeros((64, 128), F32)
     for g in range(BEFORE):
         second_total = field_step(g, second_total)
-
-    pl.semaphore_wait(barrier, len(LINE) + len(PLANE) + 4)
-
-    pair_depth = send(
-        depth_parts.at[pl.ds((1 - core) * 4, 4)], depth_sib, pair_send.at[0], pair_recv.at[0], sibling
-    )
-
-    for g in range(BEFORE, BEFORE + 1):
-        second_total = field_step(g, second_total)
-
-    pair_depth.wait_recv()
-    depth_sum[...] = depth_parts[pl.ds(core * 4, 4)] + depth_sib[...]
-    for dx, dy in PLANE:
-        to = in_plane(dx, dy)
-        send(depth_sum.at[to // NY], depth_plane.at[gx], many_send.at[0], many_recv.at[0], at_plane(to))
-    depth_plane[gx] = depth_sum[x]
-
-    for g in range(BEFORE + 1, 8):
+    pl.when(jnp.logical_not(early))(meet)
+    for g in range(BEFORE, 4):
         second_total = field_step(g, second_total)
     rows_second[...] = second_total
 
@@ -315,14 +335,12 @@
     first_pack[0, 0:10, :] = packed[0:10, :]
     first_pack[1, 0:10, :] = packed[10:20, :]
     second_pack[0:20, :] = pack(rows_second[...])
-
-    pair_var = send(second_pack, second_var, pair_send.at[2], pair_recv.at[2], partner)
-    pair_first = send(first_pack.at[1 - core], first_sib, pair_send.at[1], pair_recv.at[1], sibling)
+    pl.when(jnp.logical_not(early))(share)
 
     def core_step(side, target, q):
         for s in range(ZC // 2):
             for t in range(2):
-                place = (z_low + HALF - OFFSET + q * ZC + s * 2 + t) % HALF
+                place = (z_low + HALF - (q * ZC + s * 2 + t)) % HALF
                 for b in range(3):
                     part = stage[pl.ds(place * 6 + 3 * side + b, 64, stride=48), :]
                     parts = [(b, part)]
@@ -339,21 +357,33 @@
             for t in range(2):
                 target[q, :, s * 2 + t] = result[:, t * 128 : t * 128 + 128].reshape(GX, 8, 128)
 
-    pair_core = []
     for q in range(CHUNKS):
         core_step(1 - core, core_away, q)
-        pair_core.append(send(
-                core_away.at[q, :, :, pl.ds(0, 7)],
-                core_sib.at[q, :, :, pl.ds(0, 7)],
-                core_send.at[q],
-                core_recv.at[q],
-                sibling,
-            ))
+        pl.when(jnp.logical_not(early))(lambda q=q: away(q))
+    @pl.when(early)
+    def _():
+        meet()
+        share()
+        for q in range(CHUNKS):
+            away(q)
+
     for q in range(CHUNKS):
         core_step(core, core_own, q)
 
+    all_of(first_sib, pair_recv.at[0]).wait_recv()
+    first_sum[...] = first_pack[core] + first_sib[...]
+    for dz in LINE:
+        send(
+            first_sum.at[pl.ds(0, 8)],
+            first_line.at[z],
+            many_send.at[1],
+            many_recv.at[1],
+            at_line((z + dz) % NZ),
+        )
+    first_line[z] = first_sum[0:8, :]
+
     for q in range(CHUNKS):
-        pair_core[q].wait_recv()
+        all_of(core_sib.at[q, :, :, pl.ds(0, 7)], core_recv.at[q]).wait_recv()
         core_sum[q] = core_own[q] + core_sib[q]
         for dx, dy in PLANE:
             to = in_plane(dx, dy)
@@ -366,19 +396,7 @@
             )
         core_plane[q, gx] = core_sum[q, gx]
 
-    pair_first.wait_recv()
-    first_sum[...] = first_pack[core] + first_sib[...]
-    for dz in LINE:
-        send(
-            first_sum.at[pl.ds(0, 8)],
-            first_line.at[z],
-            many_send.at[1],
-            many_recv.at[1],
-            at_line((z + dz) % NZ),
-        )
-    first_line[z] = first_sum[0:8, :]
-
-    all_of(depth_plane.at[pl.ds(0, 15)], many_recv.at[0]).wait_recv()
+    all_of(depth_plane.at[pl.ds(0, 31)], many_recv.at[0]).wait_recv()
     depth_tile[0:5, :] = jnp.sum(depth_plane[...], axis=0)[0:5, :]
     depth_tile[5:8, :] = first_sum[8:11, :]
     for dz in LINE:
@@ -390,14 +408,14 @@
         core_tiles[q] = jnp.sum(core_plane[q], axis=0)
         for far in (0, 1):
             for s in range(ZC):
-                ahead = q * ZC + s - OFFSET
-                if ahead == 0 and far:
+                behind = q * ZC + s
+                if behind == 0 and far:
                     continue
-                to = (z + ahead + HALF * (1 - far) + NZ) % NZ
+                to = (z + HALF * (1 + far) - behind) % NZ
                 send(core_tiles.at[q, s], core_line.at[z], many_send.at[3], many_recv.at[3], at_line(to))
         if q == 0:
-            core_line[z] = core_tiles[0, OFFSET]
-            pair_var.wait_recv()
+            core_line[z] = core_tiles[0, 0]
+            all_of(second_var, pair_recv.at[1]).wait_recv()
             second_sum[...] = second_pack[...] + second_var[...]
             for dx, dy in PLANE:
                 send(
@@ -409,7 +427,6 @@
                 )
             second_plane[gx] = second_sum[...]
 
-    mine = core * NX + x
     all_of(depth_line.at[pl.ds(0, 15)], many_recv.at[2]).wait_recv()
     depth_line_sum = jnp.sum(depth_line[...], axis=0)
     depth_all[mine] = depth_line_sum
@@ -420,7 +437,7 @@
     first_whole[core, 0:8, :] = jnp.sum(first_line[...], axis=0)
     first_whole[core, 8:16, :] = pltpu.roll(depth_line_sum, 3, 0)
     back_first = send(
-        first_whole.at[core], first_whole.at[core], pair_send.at[3], pair_recv.at[3], sibling
+        first_whole.at[core], first_whole.at[core], pair_send.at[2], pair_recv.at[2], sibling
     )
 
     all_of(second_plane.at[pl.ds(0, 15)], many_recv.at[4]).wait_recv()
@@ -469,12 +486,16 @@
     for g in range(8):
         out_depth[5 * g : 5 * g + 5, :] = depth_all[g, 0:5, :]
 
-    for copy in pair_core + [pair_depth, pair_first, pair_var, back_first]:
-        copy.wait_send()
+    back_first.wait_send()
+    all_of(first_sib, pair_send.at[0]).wait_send()
+    all_of(second_var, pair_send.at[1]).wait_send()
+    for q in range(CHUNKS):
+        all_of(core_sib.at[q, :, :, pl.ds(0, 7)], core_send.at[q]).wait_send()
     for q in range(CHUNKS):
         all_of(core_sum.at[q, pl.ds(0, 15), :, pl.ds(0, 7)], plane_send.at[q]).wait_send()
-    for i, ref in enumerate((depth_plane, first_line, depth_line, core_line, second_plane)):
-        all_of(ref.at[pl.ds(0, 15)], many_send.at[i]).wait_send()
+    all_of(depth_plane.at[pl.ds(0, 31)], many_send.at[0]).wait_send()
+    for i, ref in enumerate((first_line, depth_line, core_line, second_plane)):
+        all_of(ref.at[pl.ds(0, 15)], many_send.at[i + 1]).wait_send()
     all_of(depth_all.at[pl.ds(0, 7)], many_send.at[5]).wait_send()
 
 
@@ -537,9 +558,7 @@
             pltpu.VMEM((CHUNKS, ZC, 8, 128), F32),
             pltpu.VMEM((NZ, 8, 128), F32),
             pltpu.VMEM((8, 8, 128), F32),
-            pltpu.VMEM((4, 8, 128), F32),
-            pltpu.VMEM((4, 8, 128), F32),
-            pltpu.VMEM((GX, 8, 128), F32),
+            pltpu.VMEM((2 * GX, 8, 128), F32),
             pltpu.VMEM((8, 128), F32),
             pltpu.VMEM((NZ, 8, 128), F32),
             pltpu.VMEM((8, 8, 128), F32),
@@ -554,8 +573,8 @@
             pltpu.VMEM((GX, 24, 128), F32),
             dma((8,)),
             dma((LOADS,)),
-            dma((4,)),
-            dma((4,)),
+            dma((3,)),
+            dma((3,)),
             dma((CHUNKS,)),
             dma((CHUNKS,)),
             dma((CHUNKS,)),

time: 36.7 us -> 35.5 us (0.967)
  Pallas kernels: 35.8 us -> 34.4 us
    pallas_call x1, Pallas kernels: 34.4 us -> 33 us  [on_device(): pl.pallas_call(kernel, name='tucker', out_shape=shapes, in_specs=[pl.Bloc...]
where the time goes in v4:
time: 35.5 us; the launch traced here: 35.1 us
  Pallas kernels  34.4 us (97%)
  between operations  0.64 us (2%)
    pallas_call x1, Pallas kernels, on_device(): pl.pallas_call(kernel, name='tucker', out_shape=shapes, in_specs=[pl.Bloc...  33 us
    pallas_call x1, Pallas kernels, on_device(): pl.pallas_call(finish, name='finish', out_shape=shapes, in_specs=[vmem] *...  1.39 us

profile of v4, /device:TPU:1, one launch (start us, length us, event | category | flops | bytes accessed | tf_op | source)
XLA Modules:
  0.0 35.1 jit_solution(15579020954629991594)
XLA Ops:
  0.6 33.0 %tucker.1 = (f32[40,64]{1,0:T(8,128)}, f32[40,64]{1,0:T(8,128)}, f32[40,128]{1,0:T(8,128)}, f32[3,3,2,48]{3,2,1,0:T(2,128)}) custom-call(bf16[2,64,64,128]{3,2,1,0:T(8,128)(2,1)} %field.1, bf16[40,64]{1,0:T(8,128)(2,1)} %bitcast.11, bf16[40,64]{1,0:T(8,128)(2,1)} %bitcast.12, bf16[40,128]{1,0:T(8,128)(2,1)} %bitcast.13, bf16[2,40]{1,0:T(2,128)(2,1)} %probe_vars_hbm.1, ...), custom_call_target="tpu_custom_call" | custom-call | flops 2000000000 | bytes 3000000 | tf_op jit(solution)/shard_map/tucker/pallas_call | solution.py:526
  33.7 1.4 %finish.1 = (f32[40,64]{1,0:T(8,128)}, f32[40,64]{1,0:T(8,128)}, f32[40,128]{1,0:T(8,128)}, f32[3,3,2,48]{3,2,1,0:T(2,128)}) custom-call(f32[40,64]{1,0:T(8,128)} %get-tuple-element.12.refs_0_, f32[40,64]{1,0:T(8,128)} %get-tuple-element.13.refs_1_, f32[40,128]{1,0:T(8,128)} %get-tuple-element.14.refs_2_, f32[3,3,2,48]{3,2,1,0:T(2,128)} %get-tuple-element.15.refs_3_), custom_call_target="tpu_custom_call" | custom-call | tf_op jit(solution)/shard_map/finish/pallas_call | solution.py:600
